TPU v7x, 32 devices: a whole 2x2x4 slice. The times are simulated.
32 devices in a mesh: gx: 4 (over y, core), gy: 4 (over z), gz: 2 (over x).
Axes of the slice: x: 2, y: 2, z: 4, core: 2. Of those that a mesh axis runs over, the one named last changes fastest.
Arguments:
- inputs: bfloat16 [64, 16, 32, 256], P(None, 'gx', 'gy', 'gz'), may hold values from -6 to 6
- weight: bfloat16 [4, 4, 4, 64, 32], replicated, may hold values from -0.25 to 0.25
- cotangent: bfloat16 [2, 2, 2, 32, 16, 32, 256], P(None, None, None, None, 'gx', 'gy', 'gz'), may hold values from -3 to 3
Outputs:
- upsampled: bfloat16 [2, 2, 2, 32, 16, 32, 256], P(None, None, None, None, 'gx', 'gy', 'gz')
- input_grad: bfloat16 [64, 16, 32, 256], P(None, 'gx', 'gy', 'gz')
- weight_grad: float32 [4, 4, 4, 64, 32], replicated
All inputs are finite; a program needn't handle non-finite values.
Results may differ from a plain program's by a relative error of at most 0.0018.
Values may be sent and summed in bfloat16 or wider, within the bound.
A program may use at most 192 MiB of HBM per device.

v0:
```python
import functools
import math

import jax
import jax.numpy as jnp
from jax import lax
from jax.experimental import pallas as pl
from jax.experimental.pallas import tpu as pltpu
from jax.sharding import PartitionSpec as P

TAPS = ((1, 3), (2, 0))
G_OFF = ((0, 1), (1, 0))
IN_SHIFT = ((0, -1), (0, 1))
PAIRS = [(p, h) for p in (0, 1) for h in (0, 1)]


MESH = pl.DeviceIdType.MESH


def dot(a, b):
    return jnp.dot(a, b, preferred_element_type=jnp.float32)


def dot_nt(a, b):
    return lax.dot_general(a, b, (((1,), (1,)), ((), ())), preferred_element_type=jnp.float32)


def fused_kernel(
    streams,
    factor,
    in_ref,
    g_ref,
    w_ref,
    up_ref,
    ig_ref,
    out_ref,
    ext_ref,
    gext_ref,
    zin_ref,
    zg_ref,
    pack_in,
    pack_g,
    face_in,
    face_g,
    wf_ref,
    wi_ref,
    total,
    landed,
    gathered,
    send_sem,
    recv_sem,
):
    cells_x, cells_y, in_ch, cells_z = in_ref.shape
    out_ch = g_ref.shape[3] // 2
    wide = zin_ref.shape[-1]
    row = cells_y + 2
    count_x, count_y = lax.axis_size("gx"), lax.axis_size("gy")
    me_x, me_y, me_z = lax.axis_index("gx"), lax.axis_index("gy"), lax.axis_index("gz")
    to_x = (lax.rem(me_x + count_x - 1, count_x), lax.rem(me_x + 1, count_x))
    to_y = (lax.rem(me_y + count_y - 1, count_y), lax.rem(me_y + 1, count_y))
    other_z = {"gz": 1 - me_z}

    groups = {}
    for stage in streams[0]:
        sides = [lax.rem(lax.div(lax.axis_index(axis), bit), 2) for axis, bit in stage]
        own = sum(side << i for i, side in enumerate(sides))
        partners = []
        for change in range(1, 1 << len(stage)):
            device, number = {}, own
            for i, (axis, bit) in enumerate(stage):
                if (change >> i) % 2:
                    step = 1 - 2 * sides[i]
                    device[axis] = device.get(axis, lax.axis_index(axis)) + bit * step
                    number = number + (step << i)
            partners.append((device, number))
        groups[stage] = (own, partners)

    greeted = [{"gx": x} for x in to_x] + [{"gy": y} for y in to_y]
    greeted += [{"gx": x, "gy": y} for x in to_x for y in to_y] + [other_z]
    greeted += [device for _, partners in groups.values() for device, _ in partners]
    barrier = pltpu.get_barrier_semaphore()
    for device in greeted:
        pl.semaphore_signal(barrier, inc=1, device_id=device, device_id_type=MESH)
    pl.semaphore_wait(barrier, len(greeted))

    used = [0]

    def send(src, dst, device):
        n = used[0]
        used[0] += 1
        copy = pltpu.make_async_remote_copy(
            src_ref=src,
            dst_ref=dst,
            send_sem=send_sem.at[n],
            recv_sem=recv_sem.at[n],
            device_id=device,
            device_id_type=MESH,
        )
        copy.start()
        return copy

    inner_x, inner_y = pl.ds(1, cells_x), pl.ds(1, cells_y)
    edge_x, edge_y = (0, cells_x - 1), (0, cells_y - 1)
    spot_x, spot_y = (cells_x + 1, 0), (cells_y + 1, 0)
    over_in, over_g = [], []
    for i in (0, 1):
        over_in.append(
            send(in_ref.at[edge_x[i]], ext_ref.at[spot_x[i], inner_y], {"gx": to_x[i]})
        )
        over_in.append(
            send(in_ref.at[:, edge_y[i]], ext_ref.at[inner_x, spot_y[i]], {"gy": to_y[i]})
        )
        for j in (0, 1):
            over_in.append(
                send(
                    in_ref.at[edge_x[i], edge_y[j]],
                    ext_ref.at[spot_x[i], spot_y[j]],
                    {"gx": to_x[i], "gy": to_y[j]},
                )
            )
    far_x, far_y = (cells_x, 0), (cells_y, 0)
    for px in (0, 1):
        for py in (0, 1):
            n = px * 2 + py
            own_x, own_y = pl.ds(px, cells_x), pl.ds(py, cells_y)
            over_g.append(
                send(
                    g_ref.at[edge_x[px], :, n],
                    gext_ref.at[far_x[px], own_y, n],
                    {"gx": to_x[px]},
                )
            )
            over_g.append(
                send(
                    g_ref.at[:, edge_y[py], n],
                    gext_ref.at[own_x, far_y[py], n],
                    {"gy": to_y[py]},
                )
            )
            over_g.append(
                send(
                    g_ref.at[edge_x[px], edge_y[py], n],
                    gext_ref.at[far_x[px], far_y[py], n],
                    {"gx": to_x[px], "gy": to_y[py]},
                )
            )

    ext_ref[1 : cells_x + 1, 1 : cells_y + 1] = in_ref[...]
    for px in (0, 1):
        for py in (0, 1):
            n = px * 2 + py
            gext_ref[px : px + cells_x, py : py + cells_y, n] = g_ref[:, :, n]
    zin_ref[me_z] = jnp.zeros_like(zin_ref[0])
    zg_ref[1 - me_z] = jnp.zeros_like(zg_ref[0])

    source = (1 - me_z) * (cells_z - 1)
    half = pl.ds(pl.multiple_of((1 - me_z) * out_ch, out_ch), out_ch)

    def pack(dst, load, spots, stride):
        lane = lax.broadcasted_iota(jnp.int32, dst.shape, 1)
        held = dst[...]
        for x, y in spots:
            spot = x * stride + y
            value = load(x, y).astype(jnp.float32)
            turned = pltpu.roll(value, lax.rem(spot + wide - source, wide), 1)
            held = jnp.where(lane == spot, turned, held)
        dst[...] = held

    def load_in(x, y):
        return ext_ref[x, y]

    def load_g(x, y):
        return gext_ref[x, y, :, half, :].reshape((4 * out_ch, cells_z))

    inside = [(x, y) for x in range(1, cells_x + 1) for y in range(1, cells_y + 1)]
    around = [
        (x, y) for x in range(cells_x + 2) for y in range(cells_y + 2) if (x, y) not in inside
    ]
    inside_g = [(x, y) for x in range(1, cells_x) for y in range(1, cells_y)]
    around_g = [
        (x, y) for x in range(cells_x + 1) for y in range(cells_y + 1) if (x, y) not in inside_g
    ]
    pack_in[...] = jnp.zeros_like(pack_in)
    pack_g[...] = jnp.zeros_like(pack_g)
    pack(pack_in, load_in, inside, row)

    for px in (0, 1):
        for py in (0, 1):
            for pz, hz in PAIRS:
                wf_ref[px * 2 + py, pl.ds((2 * pz + hz) * out_ch, out_ch), :] = jnp.concatenate(
                    [
                        w_ref[TAPS[px][hx], TAPS[py][hy], TAPS[pz][hz]]
                        for hx in (0, 1)
                        for hy in (0, 1)
                    ],
                    axis=1,
                )
    for pz in (0, 1):
        rows = [
            jnp.concatenate(
                [w_ref[TAPS[px][hx], TAPS[py][hy], TAPS[pz][hz]] for hz in (0, 1)], axis=1
            )
            for px, hx in PAIRS
            for py, hy in PAIRS
        ]
        stacked = jnp.concatenate(rows, axis=0).astype(jnp.float32)
        wi_ref[pz] = stacked.T.astype(jnp.bfloat16)
    pack(pack_g, load_g, inside_g, row - 1)

    for copy in over_in:
        copy.wait()
    pack(pack_in, load_in, around, row)
    face_in[...] = pack_in[...].astype(jnp.bfloat16)
    over_z_in = send(face_in, zin_ref.at[me_z], other_z)

    lane = lax.broadcasted_iota(jnp.int32, (in_ch, cells_z), 1)
    first = lane == 0
    last = lane == cells_z - 1

    def rolled(value, amount):
        return pltpu.roll(value, amount % value.shape[-1], 1)

    over_z_in.wait()

    for px in (0, 1):
        for py in (0, 1):
            n = px * 2 + py
            edges = []
            for pz in (0, 1):
                packed = zin_ref[pz].astype(jnp.float32)
                rows = []
                for hx in (0, 1):
                    for hy in (0, 1):
                        spot = (1 + IN_SHIFT[px][hx]) * row + 1 + IN_SHIFT[py][hy]
                        rows.append(rolled(packed, -spot))
                stacked = jnp.concatenate(rows, axis=0).astype(jnp.bfloat16)
                edges.append(dot(wf_ref[n, pl.ds((2 * pz + 1) * out_ch, out_ch), :], stacked))
            for x in range(cells_x):
                rows = []
                for hx in (0, 1):
                    for hy in (0, 1):
                        rows.append(
                            jnp.concatenate(
                                [
                                    ext_ref[x + 1 + IN_SHIFT[px][hx], y + 1 + IN_SHIFT[py][hy]]
                                    for y in range(cells_y)
                                ],
                                axis=1,
                            )
                        )
                product = dot(wf_ref[n], jnp.concatenate(rows, axis=0))
                for y in range(cells_y):
                    cols = slice(y * cells_z, (y + 1) * cells_z)
                    spot = x * row + y
                    even = product[:out_ch, cols] + jnp.where(
                        first[:out_ch],
                        rolled(edges[0], -spot),
                        rolled(product[out_ch : 2 * out_ch, cols], 1),
                    )
                    odd = product[2 * out_ch : 3 * out_ch, cols] + jnp.where(
                        last[:out_ch],
                        rolled(edges[1], cells_z - 1 - spot),
                        rolled(product[3 * out_ch :, cols], -1),
                    )
                    up_ref[x, y, n, :out_ch] = even.astype(jnp.bfloat16)
                    up_ref[x, y, n, out_ch:] = odd.astype(jnp.bfloat16)

    for copy in over_g:
        copy.wait()
    pack(pack_g, load_g, around_g, row - 1)
    face_g[...] = pack_g[...].astype(jnp.bfloat16)
    over_z_g = send(face_g, zg_ref.at[1 - me_z], other_z)

    def gradients(x, pz):
        rows = []
        for px, hx in PAIRS:
            for py, hy in PAIRS:
                rows.append(
                    jnp.concatenate(
                        [
                            gext_ref[
                                x + G_OFF[px][hx],
                                y + G_OFF[py][hy],
                                px * 2 + py,
                                pl.ds(pz * out_ch, out_ch),
                                :,
                            ]
                            for y in range(cells_y)
                        ],
                        axis=1,
                    )
                )
        return jnp.concatenate(rows, axis=0)

    each = total.shape[0] // len(streams)
    begin = [j * each for j in range(len(streams))]
    length = [each for _ in streams]
    filled = [j * each for j in range(len(streams))]
    kept = [[] for _ in streams]
    flying = [None for _ in streams]

    def scatter(j, stage):
        own, partners = groups[stage]
        size = length[j] // (len(partners) + 1)
        copies = []
        for device, number in partners:
            give = pl.multiple_of(begin[j] + number * size, 8)
            area = pl.ds(filled[j], size)
            filled[j] += size
            copies.append((send(total.at[pl.ds(give, size)], landed.at[area], device), area))
        begin[j] = pl.multiple_of(begin[j] + own * size, 8)
        length[j] = size
        kept[j].append(begin[j])
        flying[j] = copies

    def settle(j):
        mine = pl.ds(begin[j], length[j])
        value = total[mine, :]
        for copy, area in flying[j]:
            copy.wait()
            value = value + landed[area, :]
        total[mine, :] = value

    def gather(j, depth):
        size = length[j]
        mine = pl.ds(kept[j][depth], size)
        flying[j] = [
            send(gathered.at[mine], gathered.at[mine], device)
            for device, _ in groups[streams[j][depth]][1]
        ]
        length[j] = size * (len(flying[j]) + 1)

    def arrive(j):
        for copy in flying[j]:
            copy.wait()

    half_rows = 16 * out_ch
    for pz in (0, 1):
        packed = zin_ref[pz].astype(jnp.float32)
        for x in range(cells_x):
            shifted = []
            for y in range(cells_y):
                here = ext_ref[x + 1, y + 1]
                spot = (x + 1) * row + y + 1
                if pz == 0:
                    near = jnp.where(
                        first, rolled(packed, -spot), rolled(here.astype(jnp.float32), 1)
                    )
                else:
                    near = jnp.where(
                        last,
                        rolled(packed, cells_z - 1 - spot),
                        rolled(here.astype(jnp.float32), -1),
                    )
                shifted.append(jnp.concatenate([here, near.astype(jnp.bfloat16)], axis=0))
            part = dot_nt(gradients(x, pz), jnp.concatenate(shifted, axis=1))
            spots = pl.ds(pz * half_rows, half_rows)
            total[spots, :] = part if x == 0 else total[spots, :] + part
        if len(streams) == 2:
            scatter(pz, streams[pz][0])
    if len(streams) == 1:
        scatter(0, streams[0][0])

    over_z_g.wait()
    edge_ig = []
    for pz in (0, 1):
        rows = []
        for px, hx in PAIRS:
            for py, hy in PAIRS:
                packed = zg_ref[pz, pl.ds((px * 2 + py) * out_ch, out_ch), :].astype(jnp.float32)
                rows.append(rolled(packed, -(G_OFF[px][hx] * (row - 1) + G_OFF[py][hy])))
        stacked = jnp.concatenate(rows, axis=0).astype(jnp.bfloat16)
        edge_ig.append(dot(wi_ref[pz, in_ch : 2 * in_ch, :], stacked))

    def input_row(x):
        parts = [[], []]
        for pz in (0, 1):
            product = dot(wi_ref[pz], gradients(x, pz))
            for y in range(cells_y):
                cols = slice(y * cells_z, (y + 1) * cells_z)
                spot = x * (row - 1) + y
                if pz == 0:
                    far = jnp.where(
                        last,
                        rolled(edge_ig[0], cells_z - 1 - spot),
                        rolled(product[in_ch:, cols], -1),
                    )
                else:
                    far = jnp.where(
                        first, rolled(edge_ig[1], -spot), rolled(product[in_ch:, cols], 1)
                    )
                parts[pz].append(product[:in_ch, cols] + far)
        for y in range(cells_y):
            ig_ref[x, y] = (parts[0][y] + parts[1][y]).astype(jnp.bfloat16)

    left = list(range(cells_x))

    def compute_some():
        if left:
            input_row(left.pop(0))

    stages = len(streams[0])
    everyone = range(len(streams))
    for depth in range(1, stages):
        compute_some()
        for j in everyone:
            settle(j)
            scatter(j, streams[j][depth])
    compute_some()
    for j in everyone:
        settle(j)
        mine = pl.ds(begin[j], length[j])
        gathered[mine, :] = total[mine, :]
        gather(j, stages - 1)
    for depth in reversed(range(stages - 1)):
        compute_some()
        for j in everyone:
            arrive(j)
            gather(j, depth)
    while left:
        compute_some()
    for j in everyone:
        arrive(j)
        for pz in (0, 1):
            if len(streams) == 2 and pz != j:
                continue
            for a, (px, hx) in enumerate(PAIRS):
                for b, (py, hy) in enumerate(PAIRS):
                    spots = pl.ds(((pz * 4 + a) * 4 + b) * out_ch, out_ch)
                    block = gathered[spots, :] * factor
                    for hz in (0, 1):
                        out_ref[TAPS[px][hx], TAPS[py][hy], TAPS[pz][hz]] = block[
                            :, hz * in_ch : (hz + 1) * in_ch
                        ]


def reduce_plan(rows):
    sizes = {axis: lax.axis_size(axis) for axis in ("gz", "gx", "gy")}
    bits = {
        axis: [(axis, 1 << bit) for bit in range(size.bit_length() - 1)]
        for axis, size in sizes.items()
    }
    plane = tuple(bits["gz"] + bits["gx"][1:])
    lines = [tuple(bits["gy"][i : i + 2]) for i in range(0, len(bits["gy"]), 2)]
    core = tuple(bits["gx"][:1])
    streams = [[core, plane] + lines, [core] + lines + [plane]]
    return streams[: max(1, min(2, rows // (8 * math.prod(sizes.values()))))]


def body(inputs, weight, cotangent):
    in_ch, cells_x, cells_y, cells_z = inputs.shape
    out_ch = weight.shape[4]
    cells = inputs.transpose(1, 2, 0, 3)
    grads = cotangent.transpose(4, 5, 0, 1, 2, 3, 6).reshape(
        (cells_x, cells_y, 4, 2 * out_ch, cells_z)
    )
    taps = weight.transpose(0, 1, 2, 4, 3)
    vmem = pl.BlockSpec(memory_space=pltpu.VMEM)
    all_cells = (
        cells_x
        * lax.axis_size("gx")
        * cells_y
        * lax.axis_size("gy")
        * cells_z
        * lax.axis_size("gz")
    )
    rows = 32 * out_ch
    plan = reduce_plan(rows)
    exchanged = sum((1 << len(stage)) - 1 for stage in plan[0])
    copies = 22 + 2 * len(plan) * exchanged
    up, ig, total = pl.pallas_call(
        functools.partial(fused_kernel, plan, 1.0 / math.sqrt(all_cells)),
        out_shape=(
            jax.ShapeDtypeStruct((cells_x, cells_y, 4, 2 * out_ch, cells_z), jnp.bfloat16),
            jax.ShapeDtypeStruct((cells_x, cells_y, in_ch, cells_z), jnp.bfloat16),
            jax.ShapeDtypeStruct((4, 4, 4, out_ch, in_ch), jnp.float32),
        ),
        in_specs=[vmem] * 3,
        out_specs=[vmem] * 3,
        scratch_shapes=[
            pltpu.VMEM((cells_x + 2, cells_y + 2, in_ch, cells_z), jnp.bfloat16),
            pltpu.VMEM((cells_x + 1, cells_y + 1, 4, 2 * out_ch, cells_z), jnp.bfloat16),
            pltpu.VMEM((2, in_ch, 128), jnp.bfloat16),
            pltpu.VMEM((2, 4 * out_ch, 128), jnp.bfloat16),
            pltpu.VMEM((in_ch, 128), jnp.float32),
            pltpu.VMEM((4 * out_ch, 128), jnp.float32),
            pltpu.VMEM((in_ch, 128), jnp.bfloat16),
            pltpu.VMEM((4 * out_ch, 128), jnp.bfloat16),
            pltpu.VMEM((4, 4 * out_ch, 4 * in_ch), jnp.bfloat16),
            pltpu.VMEM((2, 2 * in_ch, 16 * out_ch), jnp.bfloat16),
            pltpu.VMEM((rows, 2 * in_ch), jnp.float32),
            pltpu.VMEM((rows, 2 * in_ch), jnp.float32),
            pltpu.VMEM((rows, 2 * in_ch), jnp.float32),
            pltpu.SemaphoreType.DMA((copies,)),
            pltpu.SemaphoreType.DMA((copies,)),
        ],
        compiler_params=pltpu.CompilerParams(
            collective_id=0, has_side_effects=True, vmem_limit_bytes=48 * 1024 * 1024
        ),
    )(cells, grads, taps)
    up = up.reshape((cells_x, cells_y, 2, 2, 2, out_ch, cells_z)).transpose(2, 3, 4, 5, 0, 1, 6)
    return up, ig.transpose(2, 0, 1, 3), total.transpose(0, 1, 2, 4, 3)


def solution(mesh):
    placed = (P(None, "gx", "gy", "gz"), P(), P(None, None, None, None, "gx", "gy", "gz"))
    return jax.shard_map(
        body,
        mesh=mesh,
        in_specs=placed,
        out_specs=(P(None, None, None, None, "gx", "gy", "gz"), P(None, "gx", "gy", "gz"), P()),
        check_vma=False,
    )
```

profile of v0, /device:TPU:0, one launch (start us, length us, event | category | flops | bytes accessed | tf_op | source)
XLA Modules:
  0.0 55.4 jit_solution(4203977293594465157)
XLA Ops:
  0.6 1.2 %copy.13 = bf16[64,4,8,128]{3,0,2,1:T(8,128)(2,1)S(1)} copy(bf16[64,4,8,128]{3,2,1,0:T(8,128)(2,1)} %param.3) | data formatting | bytes 1048576 | tf_op args[0]
  1.9 0.0 copy-start
  1.9 3.8 %copy.7 = bf16[4,8,2,2,2,32,128]{6,5,4,3,2,1,0:T(8,128)(2,1)} copy(bf16[4,8,2,2,2,32,128]{6,1,0,5,4,3,2:T(8,128)(2,1)} %bitcast.18) | data formatting | bytes 4194304 | tf_op jit(solution)/shard_map/transpose | solution.py:454
  5.7 0.0 copy-done
  5.7 45.0 %shard_map.58 = (bf16[4,8,4,64,128]{4,3,2,1,0:T(8,128)(2,1)S(1)}, bf16[4,8,64,128]{3,2,1,0:T(8,128)(2,1)S(1)}, f32[4,4,4,32,64]{4,3,2,1,0:T(8,128)S(1)}) custom-call(bf16[4,8,64,128]{3,2,1,0:T(8,128)(2,1)S(1)} %bitcast.13, bf16[4,8,4,64,128]{4,3,2,1,0:T(8,128)(2,1)} %bitcast.17, bf16[4,4,4,32,64]{4,3,2,1,0:T(8,128)(2,1)S(1)} %bitcast.16), custom_call_target="tpu_custom_call" | custom-call | tf_op jit(solution)/shard_map/pallas_call | solution.py:471
  50.7 2.7 %copy.12 = bf16[4,8,2,2,2,32,128]{6,1,0,5,4,3,2:T(8,128)(2,1)} copy(bf16[4,8,2,2,2,32,128]{6,5,4,3,2,1,0:T(8,128)(2,1)S(1)} %bitcast.12) | data formatting | bytes 4194304 | tf_op jit(solution)/shard_map/reshape | solution.py:501
  53.3 1.1 %copy.9 = bf16[64,4,8,128]{3,2,1,0:T(8,128)(2,1)} copy(bf16[64,4,8,128]{3,0,2,1:T(8,128)(2,1)S(1)} %bitcast.15) | data formatting | bytes 1048576
  54.5 1.0 %copy.15 = f32[4,4,4,64,32]{3,4,2,1,0:T(8,128)} copy(f32[4,4,4,64,32]{3,4,2,1,0:T(8,128)S(1)} %bitcast.14) | data formatting | bytes 1048576
Async XLA Ops:
  1.9 3.8 %copy-start = (bf16[4,4,4,64,32]{3,4,2,1,0:T(8,128)(2,1)S(1)}, bf16[4,4,4,64,32]{3,4,2,1,0:T(8,128)(2,1)}, u32[]{:S(2)}) copy-start(bf16[4,4,4,64,32]{3,4,2,1,0:T(8,128)(2,1)} %param.4) | copy-start | bytes 786436
where the time goes:
time: 55.7 us; the launch traced here: 55.4 us
  Pallas kernels  45 us (81%)
  local copies, waits for them, and re-layouts  9.81 us (18%)
  between operations  0.65 us (1%)
    pallas_call x1, Pallas kernels, body(): pl.pallas_call(functools.partial(fused_kernel, plan, 1.0 / math.sqrt(all_...  45 us
    transpose x1, local copies, waits for them, and re-layouts, body(): cotangent.transpose(4, 5, 0, 1, 2, 3, 6)  3.78 us
    unnamed x5, local copies, waits for them, and re-layouts  3.36 us
    reshape x1, local copies, waits for them, and re-layouts, body(): up.reshape((cells_x, cells_y, 2, 2, 2, out_ch, cells_z))  2.67 us

commit v1 on v0

--- a/solution.py
+++ b/solution.py
@@ -102,7 +102,7 @@
     inner_x, inner_y = pl.ds(1, cells_x), pl.ds(1, cells_y)
     edge_x, edge_y = (0, cells_x - 1), (0, cells_y - 1)
     spot_x, spot_y = (cells_x + 1, 0), (cells_y + 1, 0)
-    over_in, over_g = [], []
+    over_in = []
     for i in (0, 1):
         over_in.append(
             send(in_ref.at[edge_x[i]], ext_ref.at[spot_x[i], inner_y], {"gx": to_x[i]})
@@ -118,7 +118,47 @@
                     {"gx": to_x[i], "gy": to_y[j]},
                 )
             )
+    ext_ref[1 : cells_x + 1, 1 : cells_y + 1] = in_ref[...]
+    for px in (0, 1):
+        for py in (0, 1):
+            n = px * 2 + py
+            gext_ref[px : px + cells_x, py : py + cells_y, n] = g_ref[:, :, n]
+    zin_ref[me_z] = jnp.zeros_like(zin_ref[0])
+    zg_ref[1 - me_z] = jnp.zeros_like(zg_ref[0])
+
+    source = (1 - me_z) * (cells_z - 1)
+    half = pl.ds(pl.multiple_of((1 - me_z) * out_ch, out_ch), out_ch)
+
+    def pack(dst, load, spots, stride):
+        lane = lax.broadcasted_iota(jnp.int32, dst.shape, 1)
+        held = dst[...]
+        for x, y in spots:
+            spot = x * stride + y
+            value = load(x, y).astype(jnp.float32)
+            turned = pltpu.roll(value, lax.rem(spot + wide - source, wide), 1)
+            held = jnp.where(lane == spot, turned, held)
+        dst[...] = held
+
+    def load_in(x, y):
+        return ext_ref[x, y]
+
+    def load_g(x, y):
+        return gext_ref[x, y, :, half, :].reshape((4 * out_ch, cells_z))
+
+    inside = [(x, y) for x in range(1, cells_x + 1) for y in range(1, cells_y + 1)]
+    around = [
+        (x, y) for x in range(cells_x + 2) for y in range(cells_y + 2) if (x, y) not in inside
+    ]
+    inside_g = [(x, y) for x in range(1, cells_x) for y in range(1, cells_y)]
+    around_g = [
+        (x, y) for x in range(cells_x + 1) for y in range(cells_y + 1) if (x, y) not in inside_g
+    ]
+    pack_in[...] = jnp.zeros_like(pack_in)
+    pack_g[...] = jnp.zeros_like(pack_g)
+    pack(pack_in, load_in, inside, row)
+
     far_x, far_y = (cells_x, 0), (cells_y, 0)
+    over_g = []
     for px in (0, 1):
         for py in (0, 1):
             n = px * 2 + py
@@ -144,45 +184,6 @@
                     {"gx": to_x[px], "gy": to_y[py]},
                 )
             )
-
-    ext_ref[1 : cells_x + 1, 1 : cells_y + 1] = in_ref[...]
-    for px in (0, 1):
-        for py in (0, 1):
-            n = px * 2 + py
-            gext_ref[px : px + cells_x, py : py + cells_y, n] = g_ref[:, :, n]
-    zin_ref[me_z] = jnp.zeros_like(zin_ref[0])
-    zg_ref[1 - me_z] = jnp.zeros_like(zg_ref[0])
-
-    source = (1 - me_z) * (cells_z - 1)
-    half = pl.ds(pl.multiple_of((1 - me_z) * out_ch, out_ch), out_ch)
-
-    def pack(dst, load, spots, stride):
-        lane = lax.broadcasted_iota(jnp.int32, dst.shape, 1)
-        held = dst[...]
-        for x, y in spots:
-            spot = x * stride + y
-            value = load(x, y).astype(jnp.float32)
-            turned = pltpu.roll(value, lax.rem(spot + wide - source, wide), 1)
-            held = jnp.where(lane == spot, turned, held)
-        dst[...] = held
-
-    def load_in(x, y):
-        return ext_ref[x, y]
-
-    def load_g(x, y):
-        return gext_ref[x, y, :, half, :].reshape((4 * out_ch, cells_z))
-
-    inside = [(x, y) for x in range(1, cells_x + 1) for y in range(1, cells_y + 1)]
-    around = [
-        (x, y) for x in range(cells_x + 2) for y in range(cells_y + 2) if (x, y) not in inside
-    ]
-    inside_g = [(x, y) for x in range(1, cells_x) for y in range(1, cells_y)]
-    around_g = [
-        (x, y) for x in range(cells_x + 1) for y in range(cells_y + 1) if (x, y) not in inside_g
-    ]
-    pack_in[...] = jnp.zeros_like(pack_in)
-    pack_g[...] = jnp.zeros_like(pack_g)
-    pack(pack_in, load_in, inside, row)
 
     for px in (0, 1):
         for py in (0, 1):
@@ -267,9 +268,6 @@
 
     for copy in over_g:
         copy.wait()
-    pack(pack_g, load_g, around_g, row - 1)
-    face_g[...] = pack_g[...].astype(jnp.bfloat16)
-    over_z_g = send(face_g, zg_ref.at[1 - me_z], other_z)
 
     def gradients(x, pz):
         rows = []
@@ -361,6 +359,19 @@
     if len(streams) == 1:
         scatter(0, streams[0][0])
 
+    pack(pack_g, load_g, around_g, row - 1)
+    face_g[...] = pack_g[...].astype(jnp.bfloat16)
+    over_z_g = send(face_g, zg_ref.at[1 - me_z], other_z)
+
+    stages = len(streams[0])
+    everyone = range(len(streams))
+
+    def advance(depth):
+        for j in everyone:
+            settle(j)
+            scatter(j, streams[j][depth])
+
+    advance(1)
     over_z_g.wait()
     edge_ig = []
     for pz in (0, 1):
@@ -399,13 +410,9 @@
         if left:
             input_row(left.pop(0))
 
-    stages = len(streams[0])
-    everyone = range(len(streams))
-    for depth in range(1, stages):
+    for depth in range(2, stages):
         compute_some()
-        for j in everyone:
-            settle(j)
-            scatter(j, streams[j][depth])
+        advance(depth)
     compute_some()
     for j in everyone:
         settle(j)
@@ -495,7 +502,7 @@
             pltpu.SemaphoreType.DMA((copies,)),
         ],
         compiler_params=pltpu.CompilerParams(
-            collective_id=0, has_side_effects=True, vmem_limit_bytes=48 * 1024 * 1024
+            collective_id=0, has_side_effects=True, vmem_limit_bytes=24 * 1024 * 1024
         ),
     )(cells, grads, taps)
     up = up.reshape((cells_x, cells_y, 2, 2, 2, out_ch, cells_z)).transpose(2, 3, 4, 5, 0, 1, 6)

time: 55.7 us -> 52.6 us (0.944)
  Pallas kernels: 45 us -> 43.3 us
  local copies, waits for them, and re-layouts: 9.81 us -> 8.49 us
    pallas_call x1, Pallas kernels: 45 us -> 43.3 us  [body(): pl.pallas_call(functools.partial(fused_kernel, plan, 1.0 / math.sqrt(all_...]
    transpose x1, local copies, waits for them, and re-layouts: 3.78 us -> 2.46 us  [body(): cotangent.transpose(4, 5, 0, 1, 2, 3, 6)]
where the time goes in v1:
time: 52.6 us; the launch traced here: 52.4 us
  Pallas kernels  43.3 us (82%)
  local copies, waits for them, and re-layouts  8.49 us (16%)
  between operations  0.66 us (1%)
    pallas_call x1, Pallas kernels, body(): pl.pallas_call(functools.partial(fused_kernel, plan, 1.0 / math.sqrt(all_...  43.3 us
    unnamed x5, local copies, waits for them, and re-layouts  3.36 us
    reshape x1, local copies, waits for them, and re-layouts, body(): up.reshape((cells_x, cells_y, 2, 2, 2, out_ch, cells_z))  2.67 us
    transpose x1, local copies, waits for them, and re-layouts, body(): cotangent.transpose(4, 5, 0, 1, 2, 3, 6)  2.46 us

profile of v1, /device:TPU:0, one launch (start us, length us, event | category | flops | bytes accessed | tf_op | source)
XLA Modules:
  0.0 52.4 jit_solution(5044827779191880435)
XLA Ops:
  0.6 1.2 %copy.13 = bf16[64,4,8,128]{3,0,2,1:T(8,128)(2,1)S(1)} copy(bf16[64,4,8,128]{3,2,1,0:T(8,128)(2,1)} %param.3) | data formatting | bytes 1048576 | tf_op args[0]
  1.9 0.0 copy-start
  1.9 2.5 %copy.7 = bf16[4,8,2,2,2,32,128]{6,5,4,3,2,1,0:T(8,128)(2,1)S(1)} copy(bf16[4,8,2,2,2,32,128]{6,1,0,5,4,3,2:T(8,128)(2,1)} %bitcast.18) | data formatting | bytes 4194304 | tf_op jit(solution)/shard_map/transpose | solution.py:461
  4.4 0.0 copy-done
  4.4 43.3 %shard_map.58 = (bf16[4,8,4,64,128]{4,3,2,1,0:T(8,128)(2,1)S(1)}, bf16[4,8,64,128]{3,2,1,0:T(8,128)(2,1)S(1)}, f32[4,4,4,32,64]{4,3,2,1,0:T(8,128)S(1)}) custom-call(bf16[4,8,64,128]{3,2,1,0:T(8,128)(2,1)S(1)} %bitcast.14, bf16[4,8,4,64,128]{4,3,2,1,0:T(8,128)(2,1)S(1)} %bitcast.12, bf16[4,4,4,32,64]{4,3,2,1,0:T(8,128)(2,1)S(1)} %bitcast.17), custom_call_target="tpu_custom_call" | custom-call | tf_op jit(solution)/shard_map/pallas_call | solution.py:478
  47.6 2.7 %copy.12 = bf16[4,8,2,2,2,32,128]{6,1,0,5,4,3,2:T(8,128)(2,1)} copy(bf16[4,8,2,2,2,32,128]{6,5,4,3,2,1,0:T(8,128)(2,1)S(1)} %bitcast.13) | data formatting | bytes 4194304 | tf_op jit(solution)/shard_map/reshape | solution.py:508
  50.3 1.1 %copy.9 = bf16[64,4,8,128]{3,2,1,0:T(8,128)(2,1)} copy(bf16[64,4,8,128]{3,0,2,1:T(8,128)(2,1)S(1)} %bitcast.16) | data formatting | bytes 1048576
  51.4 1.0 %copy.15 = f32[4,4,4,64,32]{3,4,2,1,0:T(8,128)} copy(f32[4,4,4,64,32]{3,4,2,1,0:T(8,128)S(1)} %bitcast.15) | data formatting | bytes 1048576
Async XLA Ops:
  1.9 2.5 %copy-start = (bf16[4,4,4,64,32]{3,4,2,1,0:T(8,128)(2,1)S(1)}, bf16[4,4,4,64,32]{3,4,2,1,0:T(8,128)(2,1)}, u32[]{:S(2)}) copy-start(bf16[4,4,4,64,32]{3,4,2,1,0:T(8,128)(2,1)} %param.4) | copy-start | bytes 786436

commit v2 on v1

--- a/solution.py
+++ b/solution.py
@@ -34,6 +34,7 @@
     up_ref,
     ig_ref,
     out_ref,
+    cell_up,
     ext_ref,
     gext_ref,
     zin_ref,
@@ -263,8 +264,8 @@
                         rolled(edges[1], cells_z - 1 - spot),
                         rolled(product[3 * out_ch :, cols], -1),
                     )
-                    up_ref[x, y, n, :out_ch] = even.astype(jnp.bfloat16)
-                    up_ref[x, y, n, out_ch:] = odd.astype(jnp.bfloat16)
+                    cell_up[x, y, n, :out_ch] = even.astype(jnp.bfloat16)
+                    cell_up[x, y, n, out_ch:] = odd.astype(jnp.bfloat16)
 
     for copy in over_g:
         copy.wait()
@@ -401,14 +402,26 @@
                         first, rolled(edge_ig[1], -spot), rolled(product[in_ch:, cols], 1)
                     )
                 parts[pz].append(product[:in_ch, cols] + far)
-        for y in range(cells_y):
-            ig_ref[x, y] = (parts[0][y] + parts[1][y]).astype(jnp.bfloat16)
-
-    left = list(range(cells_x))
+        ig_ref[:, x] = jnp.stack(
+            [parts[0][y] + parts[1][y] for y in range(cells_y)], axis=1
+        ).astype(jnp.bfloat16)
+
+    def relay_up(x):
+        for n in range(4):
+            for pz in (0, 1):
+                tiles = [
+                    cell_up[x, y, n, pl.ds(pz * out_ch, out_ch), :].astype(jnp.float32)
+                    for y in range(cells_y)
+                ]
+                up_ref[n // 2, n % 2, pz, :, x] = jnp.stack(tiles, axis=1).astype(jnp.bfloat16)
+
+    left = [functools.partial(input_row, x) for x in range(cells_x)]
+    left += [functools.partial(relay_up, x) for x in range(cells_x)]
 
     def compute_some():
-        if left:
-            input_row(left.pop(0))
+        for _ in range(2):
+            if left:
+                left.pop(0)()
 
     for depth in range(2, stages):
         compute_some()
@@ -478,13 +491,14 @@
     up, ig, total = pl.pallas_call(
         functools.partial(fused_kernel, plan, 1.0 / math.sqrt(all_cells)),
         out_shape=(
-            jax.ShapeDtypeStruct((cells_x, cells_y, 4, 2 * out_ch, cells_z), jnp.bfloat16),
-            jax.ShapeDtypeStruct((cells_x, cells_y, in_ch, cells_z), jnp.bfloat16),
+            jax.ShapeDtypeStruct(cotangent.shape, jnp.bfloat16),
+            jax.ShapeDtypeStruct(inputs.shape, jnp.bfloat16),
             jax.ShapeDtypeStruct((4, 4, 4, out_ch, in_ch), jnp.float32),
         ),
         in_specs=[vmem] * 3,
         out_specs=[vmem] * 3,
         scratch_shapes=[
+            pltpu.VMEM((cells_x, cells_y, 4, 2 * out_ch, cells_z), jnp.bfloat16),
             pltpu.VMEM((cells_x + 2, cells_y + 2, in_ch, cells_z), jnp.bfloat16),
             pltpu.VMEM((cells_x + 1, cells_y + 1, 4, 2 * out_ch, cells_z), jnp.bfloat16),
             pltpu.VMEM((2, in_ch, 128), jnp.bfloat16),
@@ -505,8 +519,7 @@
             collective_id=0, has_side_effects=True, vmem_limit_bytes=24 * 1024 * 1024
         ),
     )(cells, grads, taps)
-    up = up.reshape((cells_x, cells_y, 2, 2, 2, out_ch, cells_z)).transpose(2, 3, 4, 5, 0, 1, 6)
-    return up, ig.transpose(2, 0, 1, 3), total.transpose(0, 1, 2, 4, 3)
+    return up, ig, total.transpose(0, 1, 2, 4, 3)
 
 
 def solution(mesh):

time: 52.6 us -> 50.8 us (0.966)
  local copies, waits for them, and re-layouts: 8.49 us -> 6.8 us
    reshape x1 -> x0, local copies, waits for them, and re-layouts: 2.67 us -> none  [body(): up.reshape((cells_x, cells_y, 2, 2, 2, out_ch, cells_z))]
    unnamed x5 -> x6, local copies, waits for them, and re-layouts: 3.36 us -> 4.34 us
where the time goes in v2:
time: 50.8 us; the launch traced here: 50.6 us
  Pallas kernels  43.2 us (85%)
  local copies, waits for them, and re-layouts  6.8 us (13%)
  between operations  0.66 us (1%)
    pallas_call x1, Pallas kernels, body(): pl.pallas_call(functools.partial(fused_kernel, plan, 1.0 / math.sqrt(all_...  43.2 us
    unnamed x6, local copies, waits for them, and re-layouts  4.34 us
    transpose x1, local copies, waits for them, and re-layouts, body(): cotangent.transpose(4, 5, 0, 1, 2, 3, 6)  2.46 us

profile of v2, /device:TPU:0, one launch (start us, length us, event | category | flops | bytes accessed | tf_op | source)
XLA Modules:
  0.0 50.6 jit_solution(15780640995939930812)
XLA Ops:
  0.6 1.2 %copy.9 = bf16[64,4,8,128]{3,0,2,1:T(8,128)(2,1)S(1)} copy(bf16[64,4,8,128]{3,2,1,0:T(8,128)(2,1)} %param.3) | data formatting | bytes 1048576 | tf_op args[0]
  1.9 0.0 copy-start
  1.9 2.5 %copy.7 = bf16[4,8,2,2,2,32,128]{6,5,4,3,2,1,0:T(8,128)(2,1)S(1)} copy(bf16[4,8,2,2,2,32,128]{6,1,0,5,4,3,2:T(8,128)(2,1)} %bitcast.11) | data formatting | bytes 4194304 | tf_op jit(solution)/shard_map/transpose | solution.py:474
  4.4 0.0 copy-done
  4.4 43.2 %shard_map.58 = (bf16[2,2,2,32,4,8,128]{6,5,4,3,2,1,0:T(8,128)(2,1)S(1)}, bf16[64,4,8,128]{3,2,1,0:T(8,128)(2,1)S(1)}, f32[4,4,4,32,64]{4,3,2,1,0:T(8,128)S(1)}) custom-call(bf16[4,8,64,128]{3,2,1,0:T(8,128)(2,1)S(1)} %bitcast.8, bf16[4,8,4,64,128]{4,3,2,1,0:T(8,128)(2,1)S(1)} %bitcast.7, bf16[4,4,4,32,64]{4,3,2,1,0:T(8,128)(2,1)S(1)} %bitcast.10), custom_call_target="tpu_custom_call" | custom-call | tf_op jit(solution)/shard_map/pallas_call | solution.py:491
  47.6 1.3 %copy.13 = bf16[2,2,2,32,4,8,128]{6,5,4,3,2,1,0:T(8,128)(2,1)} copy(bf16[2,2,2,32,4,8,128]{6,5,4,3,2,1,0:T(8,128)(2,1)S(1)} %get-tuple-element.12) | data formatting | bytes 4194304
  48.9 0.8 %copy.14 = bf16[64,4,8,128]{3,2,1,0:T(8,128)(2,1)} copy(bf16[64,4,8,128]{3,2,1,0:T(8,128)(2,1)S(1)} %get-tuple-element.13) | data formatting | bytes 1048576
  49.7 1.0 %copy.15 = f32[4,4,4,64,32]{3,4,2,1,0:T(8,128)} copy(f32[4,4,4,64,32]{3,4,2,1,0:T(8,128)S(1)} %bitcast.9) | data formatting | bytes 1048576
Async XLA Ops:
  1.9 2.5 %copy-start = (bf16[4,4,4,64,32]{3,4,2,1,0:T(8,128)(2,1)S(1)}, bf16[4,4,4,64,32]{3,4,2,1,0:T(8,128)(2,1)}, u32[]{:S(2)}) copy-start(bf16[4,4,4,64,32]{3,4,2,1,0:T(8,128)(2,1)} %param.4) | copy-start | bytes 786436
